TPU v7x, 32 devices: a whole 2x2x4 slice. The times are simulated.
32 devices in a mesh: hst: 8 (over y, x, core), chip: 4 (over z).
Axes of the slice: x: 2, y: 2, z: 4, core: 2. Of those that a mesh axis runs over, the one named last changes fastest.
Arguments:
- points: bfloat16 [16384, 1024], P(('hst', 'chip')), may hold values from -640 to 640
- assign: int32 [16384], P(('hst', 'chip')), may hold values from 0 to 1023, as said below
Outputs:
- centroids: bfloat16 [1024, 1024], P('hst', 'chip')
- nearest: float32 [16384], P(('hst', 'chip'))
Inputs may be any that keep to these rules, and one draw needn't show every extreme that they name: `assign`: cluster o * 128 + j lies in owner block o. Among the 512 points of one device at most 128 name clusters of any one owner block; in every draw one owner block gets exactly 128 points from every device.
All inputs are finite; a program needn't handle non-finite values.
Results may differ from a plain program's by a relative error of at most 0.0095.
Values may be sent and summed in bfloat16 or wider, within the bound.
A program may use at most 64 MiB of HBM per device.

v0:
```python
import jax
import jax.numpy as jnp
from jax import lax
from jax.sharding import PartitionSpec as P

K_HOST = 128
CYCLE = 8


EPSILON = 1e-06


def shifted(block, axis, distance):
    devices = range(lax.axis_size(axis))
    route = [((i - distance) % len(devices), i) for i in devices]
    return lax.ppermute(block, axis, route)


def cluster_sums(values, labels, row_count):
    stride = min(row_count, 1024)

    def one_block(offset):
        wanted = offset + jnp.arange(stride, dtype=jnp.int32)
        member = (wanted[:, None] == labels[None, :]).astype(jnp.bfloat16)
        return jnp.dot(member, values, preferred_element_type=jnp.float32)

    offsets = jnp.arange(row_count // stride, dtype=jnp.int32) * stride
    return lax.map(one_block, offsets).reshape(row_count, values.shape[1])


def body(points, assign):
    feature_count = points.shape[1]
    chip_count = lax.axis_size("chip")
    chip_index = lax.axis_index("chip")
    quarter = feature_count // chip_count
    host_points, host_labels = (
        lax.all_gather(points, "chip", axis=0, tiled=True),
        lax.all_gather(assign, "chip", axis=0, tiled=True),
    )
    columns = lax.dynamic_slice_in_dim(host_points, chip_index * quarter, quarter, 1)
    shares = lax.psum_scatter(
        cluster_sums(columns, host_labels, K_HOST * lax.axis_size("hst")),
        "hst",
        scatter_dimension=0,
        tiled=True,
    )
    squares = lax.psum(jnp.sum(shares * shares, axis=1), "chip")
    factor = lax.rsqrt(squares / feature_count + EPSILON)
    centroids = (shares * factor[:, None]).astype(jnp.bfloat16)
    own_block = lax.all_gather(centroids, "chip", axis=1, tiled=True)
    widened = points.astype(jnp.float32)
    unit_points = (
        widened * lax.rsqrt(jnp.mean(widened * widened, axis=1, keepdims=True) + EPSILON)
    ).astype(jnp.bfloat16)

    def nearest_in(candidates):
        scores = jnp.einsum(
            "pd,kd->pk", unit_points, candidates, preferred_element_type=jnp.float32
        )
        return jnp.min(2.0 - 2.0 * scores / feature_count, axis=1)

    nearest = nearest_in(own_block)
    moving = own_block
    for section_index in range(CYCLE - 1):
        moving = shifted(moving, "hst", 1)
        nearest = jnp.minimum(nearest, nearest_in(moving))
    return (centroids, nearest)


def solution(mesh):
    in_specs = (P(("hst", "chip"), None), P(("hst", "chip")))
    out_specs = (P("hst", "chip"), P(("hst", "chip")))
    return jax.shard_map(body, mesh=mesh, in_specs=in_specs, out_specs=out_specs, check_vma=False)
```

profile of v0, /device:TPU:0, one launch (start us, length us, event | category | flops | bytes accessed | tf_op | source)
XLA Modules:
  0.0 214.0 jit_solution(18349763476725671488)
XLA Ops:
  7.2 0.0 all-gather.3.cloned.1.call-start
  7.2 0.7 all-gather.3.cloned.1.call-update
  7.9 0.0 reduce-scatter.2.cloned.1.call-start
  7.9 13.7 %all-gather = s32[4,1,512]{2,1,0:T(1,128)S(1)} all-gather(s32[1,1,512]{2,1,0:T(1,128)} %bitcast.11), channel_id=1, replica_groups=mesh['hst'=8,'chip'=4] {'chip'}, dimensions={0}, use_global_device_ids=true | all-gather | bytes 10240 | tf_op jit(solution)/shard_map/all_gather | solution.py:38
  21.6 71.4 %all-gather.3.cloned.1.call-done = bf16[2048,1024]{1,0:T(8,128)(2,1)} async-done(((bf16[512,1024]{1,0:T(8,128)(2,1)}), bf16[2048,1024]{1,0:T(8,128)(2,1)}) %all-gather.3.cloned.1.call-update) | async-done | bytes 4194320 | tf_op jit(solution)/shard_map/all_gather | solution.py:37
  93.1 3.6 %fusion = f32[1024,256]{1,0:T(8,128)} fusion(s32[2048]{0:T(1024)S(1)} %bitcast.10, bf16[2048,1024]{1,0:T(8,128)(2,1)} %all-gather.3.cloned.1.call-done, s32[]{:T(128)S(6)} %select_n.3), kind=kOutput, calls=%fused_computation.1 | convolution fusion | flops 1075838976 | bytes 2105348 | tf_op jit(solution)/shard_map/while/body/eval_jaxpr/dot_general | solution.py:25
  96.7 0.0 reduce-scatter.2.cloned.1.call-update
  96.7 34.7 %reduce-scatter.2.cloned.1.call-done = f32[128,256]{1,0:T(8,128)} async-done(((f32[1024,256]{1,0:T(8,128)}), f32[128,256]{1,0:T(8,128)}) %reduce-scatter.2.cloned.1.call-update) | async-done | bytes 131088 | tf_op jit(solution)/shard_map/reduce_scatter | solution.py:41
  131.5 1.0 multiply_reduce_fusion
  132.5 11.7 %psum.7 = f32[128]{0:T(128)S(1)} all-reduce(f32[128]{0:T(128)S(1)} %multiply_reduce_fusion), channel_id=1, replica_groups=mesh['hst'=8,'chip'=4] {'chip'}, use_global_device_ids=true, to_apply=%region_2.3 | all-reduce | flops 128 | bytes 1024 | tf_op jit(solution)/shard_map/psum | solution.py:47
  144.2 1.0 multiply_convert_fusion
  145.2 0.0 copy-start.1
  145.2 13.9 %all_gather.11 = bf16[128,1024]{1,0:T(8,128)(2,1)S(1)} all-gather(bf16[128,256]{1,0:T(8,128)(2,1)S(1)} %multiply_convert_fusion), channel_id=1, replica_groups=mesh['hst'=8,'chip'=4] {'chip'}, dimensions={1}, use_global_device_ids=true | all-gather | bytes 327680 | tf_op jit(solution)/shard_map/all_gather | solution.py:50
  159.1 0.0 collective-permute-start
  159.1 6.7 %collective-permute-done = bf16[128,1024]{1,0:T(8,128)(2,1)S(1)} collective-permute-done((bf16[128,1024]{1,0:T(8,128)(2,1)S(1)}, bf16[128,1024]{1,0:T(8,128)(2,1)S(1)}, u32[]{:S(2)}, u32[]{:S(2)}) %collective-permute-start) | collective-permute-done | bytes 262176 | tf_op jit(solution)/shard_map/ppermute | solution.py:16
  165.8 6.7 %collective-permute-done.1 = bf16[128,1024]{1,0:T(8,128)(2,1)S(1)} collective-permute-done((bf16[128,1024]{1,0:T(8,128)(2,1)S(1)}, bf16[128,1024]{1,0:T(8,128)(2,1)S(1)}, u32[]{:S(2)}, u32[]{:S(2)}) %collective-permute-start.1) | collective-permute-done | bytes 262176 | tf_op jit(solution)/shard_map/ppermute | solution.py:16
  172.5 0.3 fusion.2
  172.8 6.4 %collective-permute-done.2 = bf16[128,1024]{1,0:T(8,128)(2,1)S(1)} collective-permute-done((bf16[128,1024]{1,0:T(8,128)(2,1)S(1)}, bf16[128,1024]{1,0:T(8,128)(2,1)S(1)}, u32[]{:S(2)}, u32[]{:S(2)}) %collective-permute-start.2) | collective-permute-done | bytes 262176 | tf_op jit(solution)/shard_map/ppermute | solution.py:16
  179.2 0.0 collective-permute-start.3
  179.2 0.6 fusion.12
  179.8 6.1 %collective-permute-done.3 = bf16[128,1024]{1,0:T(8,128)(2,1)S(1)} collective-permute-done((bf16[128,1024]{1,0:T(8,128)(2,1)S(1)}, bf16[128,1024]{1,0:T(8,128)(2,1)S(1)}, u32[]{:S(2)}, u32[]{:S(2)}) %collective-permute-start.3) | collective-permute-done | bytes 262176 | tf_op jit(solution)/shard_map/ppermute | solution.py:16
  185.9 0.6 fusion.13
  186.5 0.6 fusion.14
  187.0 5.5 %collective-permute-done.4 = bf16[128,1024]{1,0:T(8,128)(2,1)S(1)} collective-permute-done((bf16[128,1024]{1,0:T(8,128)(2,1)S(1)}, bf16[128,1024]{1,0:T(8,128)(2,1)S(1)}, u32[]{:S(2)}, u32[]{:S(2)}) %collective-permute-start.4) | collective-permute-done | bytes 262176 | tf_op jit(solution)/shard_map/ppermute | solution.py:16
  192.6 0.6 fusion.15
  193.2 0.6 fusion.16
  193.7 5.5 %collective-permute-done.5 = bf16[128,1024]{1,0:T(8,128)(2,1)S(1)} collective-permute-done((bf16[128,1024]{1,0:T(8,128)(2,1)S(1)}, bf16[128,1024]{1,0:T(8,128)(2,1)S(1)}, u32[]{:S(2)}, u32[]{:S(2)}) %collective-permute-start.5) | collective-permute-done | bytes 262176 | tf_op jit(solution)/shard_map/ppermute | solution.py:16
  199.3 0.6 fusion.17
  199.8 0.6 fusion.18
  200.4 5.6 %collective-permute-done.6 = bf16[128,1024]{1,0:T(8,128)(2,1)S(1)} collective-permute-done((bf16[128,1024]{1,0:T(8,128)(2,1)S(1)}, bf16[128,1024]{1,0:T(8,128)(2,1)S(1)}, u32[]{:S(2)}, u32[]{:S(2)}) %collective-permute-start.6) | collective-permute-done | bytes 262176 | tf_op jit(solution)/shard_map/ppermute | solution.py:16
  206.0 0.6 fusion.19
  206.5 0.6 minimum_minimum_fusion
  (10 shorter events, 0.0 us)
Async XLA Ops:
  7.2 85.9 %all-gather.3.cloned.1.call-start = ((), (), s32[]{:S(2)}) async-start(), calls=%async_computation.1 | async-start | bytes 5242880 | tf_op jit(solution)/shard_map/all_gather | solution.py:37
  7.9 123.6 %reduce-scatter.2.cloned.1.call-start = ((), (), s32[]{:S(2)}) async-start(), calls=%async_computation.2 | async-start | bytes 1179648 | tf_op jit(solution)/shard_map/reduce_scatter | solution.py:41
  96.7 75.8 %copy-start = (bf16[512,1024]{1,0:T(8,128)(2,1)S(1)}, bf16[512,1024]{1,0:T(8,128)(2,1)}, u32[]{:S(2)}) copy-start(bf16[512,1024]{1,0:T(8,128)(2,1)} %param.2) | copy-start | bytes 3145732
  145.2 41.3 %copy-start.1 = (bf16[128,256]{1,0:T(8,128)(2,1)}, bf16[128,256]{1,0:T(8,128)(2,1)S(1)}, u32[]{:S(2)}) copy-start(bf16[128,256]{1,0:T(8,128)(2,1)S(1)} %multiply_convert_fusion) | copy-start | bytes 196612
  159.1 6.7 %collective-permute-start = (bf16[128,1024]{1,0:T(8,128)(2,1)S(1)}, bf16[128,1024]{1,0:T(8,128)(2,1)S(1)}, u32[]{:S(2)}, u32[]{:S(2)}) collective-permute-start(bf16[128,1024]{1,0:T(8,128)(2,1)S(1)} %all_gather.11), channel_id=1, source_target_pairs={{28,0},{0,4},{4,8},{8,12},{12,16},{16,20},{20,24},{24,28},{29,1},{... | collective-permute-start | bytes 786440 | tf_op jit(solution)/shard_map/ppermute | solution.py:16
  165.8 6.7 %collective-permute-start.1 = (bf16[128,1024]{1,0:T(8,128)(2,1)S(1)}, bf16[128,1024]{1,0:T(8,128)(2,1)S(1)}, u32[]{:S(2)}, u32[]{:S(2)}) collective-permute-start(bf16[128,1024]{1,0:T(8,128)(2,1)S(1)} %collective-permute-done), channel_id=1, source_target_pairs={{28,0},{0,4},{4,8},{8,12},{12,16},{16,20},{20,24},{24,28},{29,1},{... | collective-permute-start | bytes 786440 | tf_op jit(solution)/shard_map/ppermute | solution.py:16
  172.5 6.7 %collective-permute-start.2 = (bf16[128,1024]{1,0:T(8,128)(2,1)S(1)}, bf16[128,1024]{1,0:T(8,128)(2,1)S(1)}, u32[]{:S(2)}, u32[]{:S(2)}) collective-permute-start(bf16[128,1024]{1,0:T(8,128)(2,1)S(1)} %collective-permute-done.1), channel_id=1, source_target_pairs={{28,0},{0,4},{4,8},{8,12},{12,16},{16,20},{20,24},{24,28},{29,1},{... | collective-permute-start | bytes 786440 | tf_op jit(solution)/shard_map/ppermute | solution.py:16
  179.2 6.7 %collective-permute-start.3 = (bf16[128,1024]{1,0:T(8,128)(2,1)S(1)}, bf16[128,1024]{1,0:T(8,128)(2,1)S(1)}, u32[]{:S(2)}, u32[]{:S(2)}) collective-permute-start(bf16[128,1024]{1,0:T(8,128)(2,1)S(1)} %collective-permute-done.2), channel_id=1, source_target_pairs={{28,0},{0,4},{4,8},{8,12},{12,16},{16,20},{20,24},{24,28},{29,1},{... | collective-permute-start | bytes 786440 | tf_op jit(solution)/shard_map/ppermute | solution.py:16
  185.9 6.7 %collective-permute-start.4 = (bf16[128,1024]{1,0:T(8,128)(2,1)S(1)}, bf16[128,1024]{1,0:T(8,128)(2,1)S(1)}, u32[]{:S(2)}, u32[]{:S(2)}) collective-permute-start(bf16[128,1024]{1,0:T(8,128)(2,1)S(1)} %collective-permute-done.3), channel_id=1, source_target_pairs={{28,0},{0,4},{4,8},{8,12},{12,16},{16,20},{20,24},{24,28},{29,1},{... | collective-permute-start | bytes 786440 | tf_op jit(solution)/shard_map/ppermute | solution.py:16
  192.6 6.7 %collective-permute-start.5 = (bf16[128,1024]{1,0:T(8,128)(2,1)S(1)}, bf16[128,1024]{1,0:T(8,128)(2,1)S(1)}, u32[]{:S(2)}, u32[]{:S(2)}) collective-permute-start(bf16[128,1024]{1,0:T(8,128)(2,1)S(1)} %collective-permute-done.4), channel_id=1, source_target_pairs={{28,0},{0,4},{4,8},{8,12},{12,16},{16,20},{20,24},{24,28},{29,1},{... | collective-permute-start | bytes 786440 | tf_op jit(solution)/shard_map/ppermute | solution.py:16
  199.3 6.7 %collective-permute-start.6 = (bf16[128,1024]{1,0:T(8,128)(2,1)S(1)}, bf16[128,1024]{1,0:T(8,128)(2,1)S(1)}, u32[]{:S(2)}, u32[]{:S(2)}) collective-permute-start(bf16[128,1024]{1,0:T(8,128)(2,1)S(1)} %collective-permute-done.5), channel_id=1, source_target_pairs={{28,0},{0,4},{4,8},{8,12},{12,16},{16,20},{20,24},{24,28},{29,1},{... | collective-permute-start | bytes 786440 | tf_op jit(solution)/shard_map/ppermute | solution.py:16
Sparse Core Ops, SparseCore 0:
  9.6 83.4 all-gather.2
  96.9 34.5 reduce-scatter.1
where the time goes:
time: 214 us
  waiting for transfers between devices  149 us (70%)
  blocking collectives  39.3 us (18%)
  between operations  14.1 us (7%)
  matrix products  8.23 us (4%)
  other arithmetic  2.88 us (1%)
    all_gather x1, waiting for transfers between devices, body(): lax.all_gather(points, 'chip', axis=0, tiled=True)  71.4 us
    ppermute x7, waiting for transfers between devices, shifted(): return lax.ppermute(block, axis, route)  42.5 us
    reduce_scatter x1, waiting for transfers between devices, body(): lax.psum_scatter(cluster_sums(columns, host_labels, K_HOST * lax.axis_siz...  34.7 us
    all_gather x1, blocking collectives, body(): own_block = lax.all_gather(centroids, 'chip', axis=1, tiled=True)  13.9 us
    all_gather x1, blocking collectives, body(): lax.all_gather(assign, 'chip', axis=0, tiled=True)  13.7 us
    psum x1, blocking collectives, body(): squares = lax.psum(jnp.sum(shares * shares, axis=1), 'chip')  11.7 us
    dot_general x8, matrix products, nearest_in(): jnp.einsum('pd,kd->pk', unit_points, candidates, preferred_element_type=j...  4.59 us
  transfers between devices with their start and end apart: 9, of which 9 were waited for; matrix products, arithmetic and copies ran while one was open for 2% of the time, Pallas kernels for 0%

commit v1 on v0

--- a/solution.py
+++ b/solution.py
@@ -1,6 +1,10 @@
+import functools
+
 import jax
 import jax.numpy as jnp
 from jax import lax
+from jax.experimental import pallas as pl
+from jax.experimental.pallas import tpu as pltpu
 from jax.sharding import PartitionSpec as P
 
 K_HOST = 128
@@ -8,6 +12,7 @@
 
 
 EPSILON = 1e-06
+MESH = pl.DeviceIdType.MESH
 
 
 def shifted(block, axis, distance):
@@ -28,7 +33,7 @@
     return lax.map(one_block, offsets).reshape(row_count, values.shape[1])
 
 
-def body(points, assign):
+def general_body(points, assign):
     feature_count = points.shape[1]
     chip_count = lax.axis_size("chip")
     chip_index = lax.axis_index("chip")
@@ -67,7 +72,228 @@
     return (centroids, nearest)
 
 
+QUAD = 4
+
+
+def window_kernel(
+    chips,
+    lab_ref,
+    pts_ref,
+    cent_ref,
+    near_ref,
+    sib_lab,
+    sib_pts,
+    kept,
+    out1,
+    in1,
+    out2,
+    in2,
+    grid,
+    unit_t,
+    best_out,
+    best_in,
+    core_send,
+    core_recv,
+    s1_send,
+    s1_recv,
+    s2_send,
+    s2_recv,
+    g1_send,
+    g1_recv,
+    g2_send,
+    g2_recv,
+):
+    local, features = pts_ref.shape
+    rows = K_HOST // chips
+    h = lax.axis_index("hst")
+    c = lax.axis_index("chip")
+    core = h % 2
+    quad = h // 2
+    qx, qy = quad % 2, quad // 2
+    sibling = (h + 1 - 2 * core, c)
+    quads = [quad, qy * 2 + (1 - qx), (1 - qy) * 2 + qx, (1 - qy) * 2 + (1 - qx)]
+    quad_ids = [(q * 2 + core, c) for q in quads]
+    line = [(c + d) % chips for d in range(chips)]
+    line_ids = [(h, k) for k in line]
+
+    barrier = pltpu.get_barrier_semaphore()
+    partners = [sibling] + quad_ids[1:] + line_ids[1:]
+    for partner in partners:
+        pl.semaphore_signal(barrier, inc=1, device_id=partner, device_id_type=MESH)
+    pl.semaphore_wait(barrier, len(partners))
+
+    def remote(src, dst, send, recv, device):
+        return pltpu.make_async_remote_copy(
+            src_ref=src,
+            dst_ref=dst,
+            send_sem=send,
+            recv_sem=recv,
+            device_id=device,
+            device_id_type=MESH,
+        )
+
+    lab_copy = remote(lab_ref, sib_lab, core_send.at[0], core_recv.at[0], sibling)
+    lab_copy.start()
+    pts_copy = remote(pts_ref, sib_pts, core_send.at[1], core_recv.at[1], sibling)
+    pts_copy.start()
+    lab_copy.wait_recv()
+    pts_copy.wait_recv()
+
+    order = [d % chips for d in range(1, chips + 1)]
+    row = lax.broadcasted_iota(jnp.int32, (QUAD * rows, local), 0)
+    part, within = row // rows, row % rows
+    base = jnp.zeros_like(row)
+    for r in range(QUAD):
+        base = jnp.where(part == r, (quads[r] * 2 + core) * K_HOST, base)
+    base = base + within
+    first = [[None] * QUAD for _ in range(chips)]
+    for s, d in enumerate(order):
+        wanted = base + line[d] * rows
+        mine = (wanted == lab_ref[...]).astype(jnp.bfloat16)
+        theirs = (wanted == sib_lab[...]).astype(jnp.bfloat16)
+        sums = jnp.dot(mine, pts_ref[...], preferred_element_type=jnp.float32)
+        sums += jnp.dot(theirs, sib_pts[...], preferred_element_type=jnp.float32)
+        kept[s] = sums[:rows]
+        for r in range(1, QUAD):
+            out1[s, r - 1] = sums[r * rows : (r + 1) * rows].astype(jnp.bfloat16)
+            first[s][r] = remote(
+                out1.at[s, r - 1],
+                in1.at[s, r - 1],
+                s1_send.at[s, r - 1],
+                s1_recv.at[s, r - 1],
+                quad_ids[r],
+            )
+            first[s][r].start()
+
+    step = 128
+    for side, ref in enumerate((pts_ref, sib_pts)):
+        for begin in range(0, local, step):
+            wide = ref[begin : begin + step].astype(jnp.float32)
+            mean = jnp.mean(wide * wide, axis=1, keepdims=True)
+            unit = wide * lax.rsqrt(mean + EPSILON)
+            at = side * local + begin
+            unit_t[:, at : at + step] = unit.T.astype(jnp.bfloat16)
+
+    second = [None] * chips
+    total = None
+    for s, d in enumerate(order):
+        total = kept[s]
+        for r in range(1, QUAD):
+            first[s][r].wait_recv()
+            total = total + in1[s, r - 1].astype(jnp.float32)
+        if d:
+            out2[d - 1] = total.astype(jnp.bfloat16)
+            second[d] = remote(
+                out2.at[d - 1], in2.at[d - 1], s2_send.at[d - 1], s2_recv.at[d - 1], line_ids[d]
+            )
+            second[d].start()
+    for d in range(1, chips):
+        second[d].wait_recv()
+        total = total + in2[d - 1].astype(jnp.float32)
+    mean = jnp.mean(total * total, axis=1, keepdims=True)
+    grid[0, c] = (total * lax.rsqrt(mean + EPSILON)).astype(jnp.bfloat16)
+
+    along = [None] * chips
+    for d in range(1, chips):
+        along[d] = remote(
+            grid.at[0, c], grid.at[0, c], g1_send.at[d - 1], g1_recv.at[d - 1], line_ids[d]
+        )
+        along[d].start()
+    across = [[None] * QUAD for _ in range(chips)]
+    for d in range(chips):
+        if d:
+            along[d].wait_recv()
+        k = (c + chips - d) % chips
+        for r in range(1, QUAD):
+            across[d][r] = remote(
+                grid.at[0, k], grid.at[r, k], g2_send.at[d, r - 1], g2_recv.at[d, r - 1], quad_ids[r]
+            )
+            across[d][r].start()
+
+    def best_of(r):
+        block = grid[r].reshape(K_HOST, features)
+        scores = jnp.dot(block, unit_t[...], preferred_element_type=jnp.float32)
+        return jnp.max(scores, axis=0, keepdims=True)
+
+    quarter = features // chips
+    columns = pl.ds(pl.multiple_of(c * quarter, quarter), quarter)
+    for k in range(chips):
+        cent_ref[k * rows : (k + 1) * rows, :] = grid[0, k, :, columns]
+    best = best_of(0)
+    for r in range(1, QUAD):
+        for d in range(chips):
+            across[d][r].wait_recv()
+        best = jnp.maximum(best, best_of(r))
+
+    best_out[...] = best[:, local:]
+    last = remote(best_out, best_in, core_send.at[2], core_recv.at[2], sibling)
+    last.start()
+    for s in range(chips):
+        for r in range(1, QUAD):
+            first[s][r].wait_send()
+            across[s][r].wait_send()
+    for d in range(1, chips):
+        second[d].wait_send()
+        along[d].wait_send()
+    lab_copy.wait_send()
+    pts_copy.wait_send()
+    last.wait()
+    near_ref[...] = 2.0 - 2.0 * jnp.maximum(best[:, :local], best_in[...]) / features
+
+
+def window_body(points, assign):
+    local, features = points.shape
+    chips = lax.axis_size("chip")
+    rows = K_HOST // chips
+    vmem = pl.BlockSpec(memory_space=pltpu.VMEM)
+    dma = pltpu.SemaphoreType.DMA
+    centroids, nearest = pl.pallas_call(
+        functools.partial(window_kernel, chips),
+        out_shape=(
+            jax.ShapeDtypeStruct((K_HOST, features // chips), jnp.bfloat16),
+            jax.ShapeDtypeStruct((1, local), jnp.float32),
+        ),
+        in_specs=[vmem, vmem],
+        out_specs=(vmem, vmem),
+        scratch_shapes=[
+            pltpu.VMEM((1, local), jnp.int32),
+            pltpu.VMEM((local, features), jnp.bfloat16),
+            pltpu.VMEM((chips, rows, features), jnp.float32),
+            pltpu.VMEM((chips, QUAD - 1, rows, features), jnp.bfloat16),
+            pltpu.VMEM((chips, QUAD - 1, rows, features), jnp.bfloat16),
+            pltpu.VMEM((chips - 1, rows, features), jnp.bfloat16),
+            pltpu.VMEM((chips - 1, rows, features), jnp.bfloat16),
+            pltpu.VMEM((QUAD, chips, rows, features), jnp.bfloat16),
+            pltpu.VMEM((features, 2 * local), jnp.bfloat16),
+            pltpu.VMEM((1, local), jnp.float32),
+            pltpu.VMEM((1, local), jnp.float32),
+            dma((3,)),
+            dma((3,)),
+            dma((chips, QUAD - 1)),
+            dma((chips, QUAD - 1)),
+            dma((chips - 1,)),
+            dma((chips - 1,)),
+            dma((chips - 1,)),
+            dma((chips - 1,)),
+            dma((chips, QUAD - 1)),
+            dma((chips, QUAD - 1)),
+        ],
+        compiler_params=pltpu.CompilerParams(
+            collective_id=0, has_side_effects=True, vmem_limit_bytes=48 * 1024 * 1024
+        ),
+    )(assign.reshape(1, local), points)
+    return (centroids, nearest.reshape(local))
+
+
 def solution(mesh):
+    hosts, chips = mesh.shape["hst"], mesh.shape["chip"]
+    fits = hosts == CYCLE and hosts == 2 * QUAD and chips > 1 and K_HOST % (16 * chips) == 0
     in_specs = (P(("hst", "chip"), None), P(("hst", "chip")))
     out_specs = (P("hst", "chip"), P(("hst", "chip")))
-    return jax.shard_map(body, mesh=mesh, in_specs=in_specs, out_specs=out_specs, check_vma=False)
+    return jax.shard_map(
+        window_body if fits else general_body,
+        mesh=mesh,
+        in_specs=in_specs,
+        out_specs=out_specs,
+        check_vma=False,
+    )

time: 214 us -> 43.9 us (0.21)
  waiting for transfers between devices: 149 us -> 0 us
  Pallas kernels: 0 us -> 39.9 us
  blocking collectives: 39.3 us -> 0 us
  between operations: 14.1 us -> 0.65 us
  matrix products: 8.23 us -> 0 us
  local copies, waits for them, and re-layouts: 0.01 us -> 3.11 us
  other arithmetic: 2.88 us -> 0 us
    all_gather x1 -> x0, waiting for transfers between devices: 71.4 us -> none  [body(): lax.all_gather(points, 'chip', axis=0, tiled=True)]
    ppermute x7 -> x0, waiting for transfers between devices: 42.5 us -> none  [shifted(): return lax.ppermute(block, axis, route)]
    pallas_call x0 -> x1, Pallas kernels: none -> 39.9 us  [window_body(): pl.pallas_call(functools.partial(window_kernel, chips), out_shape=(jax.Sh...]
    reduce_scatter x1 -> x0, waiting for transfers between devices: 34.7 us -> none  [body(): lax.psum_scatter(cluster_sums(columns, host_labels, K_HOST * lax.axis_siz...]
    all_gather x2 -> x0, blocking collectives: 27.6 us -> none  [the longest x1 13.9 us: body(): own_block = lax.all_gather(centroids, 'chip', axis=1, tiled=True)]
    psum x1 -> x0, blocking collectives: 11.7 us -> none  [body(): squares = lax.psum(jnp.sum(shares * shares, axis=1), 'chip')]
    dot_general x9 -> x0, matrix products: 8.23 us -> none  [the longest x8 4.59 us: nearest_in(): jnp.einsum('pd,kd->pk', unit_points, candidates, preferred_element_type=j...]
    unnamed x4 -> x6, local copies, waits for them, and re-layouts: 0.01 us -> 3.11 us
  transfers between devices with their start and end apart: 9 -> 0, of which waited for: 9 -> 0; matrix products, arithmetic and copies ran while one was open for 2% -> 0% of each run, Pallas kernels for 0% -> 0%
where the time goes in v1:
time: 43.9 us; the launch traced here: 43.7 us
  Pallas kernels  39.9 us (91%)
  local copies, waits for them, and re-layouts  3.11 us (7%)
  between operations  0.65 us (1%)
    pallas_call x1, Pallas kernels, window_body(): pl.pallas_call(functools.partial(window_kernel, chips), out_shape=(jax.Sh...  39.9 us
    unnamed x6, local copies, waits for them, and re-layouts  3.11 us

profile of v1, /device:TPU:0, one launch (start us, length us, event | category | flops | bytes accessed | tf_op | source)
XLA Modules:
  0.0 43.7 jit_solution(2302493501055577143)
XLA Ops:
  0.6 0.0 copy-start
  0.6 1.2 %copy-done = bf16[512,1024]{1,0:T(8,128)(2,1)S(1)} copy-done((bf16[512,1024]{1,0:T(8,128)(2,1)S(1)}, bf16[512,1024]{1,0:T(8,128)(2,1)}, u32[]{:S(2)}) %copy-start) | copy-done | bytes 1048600
  1.9 0.0 copy-start.1
  1.9 0.7 %copy-done.1 = s32[512]{0:T(512)S(1)} copy-done((s32[512]{0:T(512)S(1)}, s32[512]{0:T(512)}, u32[]{:S(2)}) %copy-start.1) | copy-done | bytes 2072
  2.5 39.9 %shard_map.41 = (bf16[128,256]{1,0:T(8,128)(2,1)S(1)}, f32[1,512]{1,0:T(1,128)S(1)}) custom-call(s32[1,512]{1,0:T(1,128)S(1)} %bitcast.2, bf16[512,1024]{1,0:T(8,128)(2,1)S(1)} %copy-done), custom_call_target="tpu_custom_call" | custom-call | tf_op jit(solution)/shard_map/pallas_call | solution.py:250
  42.5 0.6 %copy.6 = bf16[128,256]{1,0:T(8,128)(2,1)} copy(bf16[128,256]{1,0:T(8,128)(2,1)S(1)} %get-tuple-element.8) | data formatting | bytes 131072
  43.1 0.6 %copy.7 = f32[512]{0:T(512)} copy(f32[512]{0:T(512)S(1)} %bitcast.3) | data formatting | bytes 4096
Async XLA Ops:
  0.6 1.2 %copy-start = (bf16[512,1024]{1,0:T(8,128)(2,1)S(1)}, bf16[512,1024]{1,0:T(8,128)(2,1)}, u32[]{:S(2)}) copy-start(bf16[512,1024]{1,0:T(8,128)(2,1)} %pts_ref.1) | copy-start | bytes 3145732
  1.9 0.7 %copy-start.1 = (s32[512]{0:T(512)S(1)}, s32[512]{0:T(512)}, u32[]{:S(2)}) copy-start(s32[512]{0:T(512)} %param.3) | copy-start | bytes 6148

commit v2 on v1

v2 whole, which is shorter than its diff:
```python
import functools

import jax
import jax.numpy as jnp
from jax import lax
from jax.experimental import pallas as pl
from jax.experimental.pallas import tpu as pltpu
from jax.sharding import PartitionSpec as P

K_HOST = 128
CYCLE = 8


EPSILON = 1e-06
MESH = pl.DeviceIdType.MESH


def shifted(block, axis, distance):
    devices = range(lax.axis_size(axis))
    route = [((i - distance) % len(devices), i) for i in devices]
    return lax.ppermute(block, axis, route)


def cluster_sums(values, labels, row_count):
    stride = min(row_count, 1024)

    def one_block(offset):
        wanted = offset + jnp.arange(stride, dtype=jnp.int32)
        member = (wanted[:, None] == labels[None, :]).astype(jnp.bfloat16)
        return jnp.dot(member, values, preferred_element_type=jnp.float32)

    offsets = jnp.arange(row_count // stride, dtype=jnp.int32) * stride
    return lax.map(one_block, offsets).reshape(row_count, values.shape[1])


def general_body(points, assign):
    feature_count = points.shape[1]
    chip_count = lax.axis_size("chip")
    chip_index = lax.axis_index("chip")
    quarter = feature_count // chip_count
    host_points, host_labels = (
        lax.all_gather(points, "chip", axis=0, tiled=True),
        lax.all_gather(assign, "chip", axis=0, tiled=True),
    )
    columns = lax.dynamic_slice_in_dim(host_points, chip_index * quarter, quarter, 1)
    shares = lax.psum_scatter(
        cluster_sums(columns, host_labels, K_HOST * lax.axis_size("hst")),
        "hst",
        scatter_dimension=0,
        tiled=True,
    )
    squares = lax.psum(jnp.sum(shares * shares, axis=1), "chip")
    factor = lax.rsqrt(squares / feature_count + EPSILON)
    centroids = (shares * factor[:, None]).astype(jnp.bfloat16)
    own_block = lax.all_gather(centroids, "chip", axis=1, tiled=True)
    widened = points.astype(jnp.float32)
    unit_points = (
        widened * lax.rsqrt(jnp.mean(widened * widened, axis=1, keepdims=True) + EPSILON)
    ).astype(jnp.bfloat16)

    def nearest_in(candidates):
        scores = jnp.einsum(
            "pd,kd->pk", unit_points, candidates, preferred_element_type=jnp.float32
        )
        return jnp.min(2.0 - 2.0 * scores / feature_count, axis=1)

    nearest = nearest_in(own_block)
    moving = own_block
    for section_index in range(CYCLE - 1):
        moving = shifted(moving, "hst", 1)
        nearest = jnp.minimum(nearest, nearest_in(moving))
    return (centroids, nearest)


QUAD = 4


def window_kernel(
    chips,
    lab_hbm,
    pts_hbm,
    cent_ref,
    near_ref,
    lab,
    pts,
    sib_lab,
    sib_pts,
    sums,
    out1,
    in1,
    out2,
    in2,
    out3,
    in3,
    grid,
    unit_t,
    best_out,
    best_in,
    load_sem,
    core_send,
    core_recv,
    s1_send,
    s1_recv,
    s2_send,
    s2_recv,
    s3_send,
    s3_recv,
    g1_send,
    g1_recv,
    g2_send,
    g2_recv,
    g3_send,
    g3_recv,
):
    local, features = pts.shape
    rows = K_HOST // chips
    half = features // 2
    halves = (slice(0, half), slice(half, features))
    h = lax.axis_index("hst")
    c = lax.axis_index("chip")
    core = h % 2
    quad = h // 2
    qx, qy = quad % 2, quad // 2
    sibling = (h + 1 - 2 * core, c)
    quads = [quad, qy * 2 + (1 - qx), (1 - qy) * 2 + qx, (1 - qy) * 2 + (1 - qx)]
    x_id, y_id = [(quads[r] * 2 + core, c) for r in (1, 2)]
    line = [c, c + 1 - 2 * (c % 2), (c + 2) % 4, 3 - c]
    line_ids = [(h, k) for k in line]

    barrier = pltpu.get_barrier_semaphore()
    partners = [sibling, x_id, y_id] + line_ids[1:]
    for partner in partners:
        pl.semaphore_signal(barrier, inc=1, device_id=partner, device_id_type=MESH)
    lab_load = pltpu.make_async_copy(lab_hbm, lab, load_sem.at[0])
    lab_load.start()
    pts_load = pltpu.make_async_copy(pts_hbm, pts, load_sem.at[1])
    pts_load.start()
    pl.semaphore_wait(barrier, len(partners))

    started = []

    def remote(src, dst, send, recv, device):
        copy = pltpu.make_async_remote_copy(
            src_ref=src,
            dst_ref=dst,
            send_sem=send,
            recv_sem=recv,
            device_id=device,
            device_id_type=MESH,
        )
        copy.start()
        started.append(copy)
        return copy

    lab_swap = remote(lab_hbm, sib_lab, core_send.at[0], core_recv.at[0], sibling)
    pts_swap = [
        remote(
            pts_hbm.at[:, halves[f]], sib_pts.at[:, halves[f]], core_send.at[1 + f], core_recv.at[1 + f], sibling
        )
        for f in range(2)
    ]

    order = (2, 3, 1, 0)
    row = lax.broadcasted_iota(jnp.int32, (QUAD * rows, local), 0)
    part, within = row // rows, row % rows
    base = jnp.zeros_like(row)
    for r in range(QUAD):
        base = jnp.where(part == r, (quads[r] * 2 + core) * K_HOST, base)
    base = base + within

    def members(s, labels):
        return (base + line[order[s]] * rows == labels[...]).astype(jnp.bfloat16)

    lab_load.wait()
    pts_load.wait()
    for s in range(chips):
        sums[s] = jnp.dot(members(s, lab), pts[...], preferred_element_type=jnp.float32)
    lab_swap.wait_recv()

    def piece(s, r, f):
        return sums[s, r * rows : (r + 1) * rows, halves[f]]

    first = [[None, None] for _ in range(chips)]
    second = [[None, None] for _ in range(chips)]
    third = [None] * chips

    def add_sibling(s):
        theirs = members(s, sib_lab)
        for f in range(2):
            if s == 0:
                pts_swap[f].wait_recv()
            sums[s, :, halves[f]] += jnp.dot(
                theirs, sib_pts[:, halves[f]], preferred_element_type=jnp.float32
            )
            near = 1 + f
            out1[s, f, 0] = piece(s, near, f).astype(jnp.bfloat16)
            out1[s, f, 1] = piece(s, 3, f).astype(jnp.bfloat16)
            if s < 2:
                send_first(s, f)

    def send_first(s, f):
        first[s][f] = remote(
            out1.at[s, f], in1.at[s, f], s1_send.at[s, f], s1_recv.at[s, f], (x_id, y_id)[f]
        )

    def send_second(s):
        for f in range(2):
            first[s][f].wait_recv()
            far = 2 - f
            out2[s, f] = (piece(s, far, f) + in1[s, f, 1].astype(jnp.float32)).astype(jnp.bfloat16)
            second[s][f] = remote(
                out2.at[s, f], in2.at[s, f], s2_send.at[s, f], s2_recv.at[s, f], (y_id, x_id)[f]
            )

    def finish(s):
        whole = []
        for f in range(2):
            second[s][f].wait_recv()
            whole.append(
                piece(s, 0, f) + in1[s, f, 0].astype(jnp.float32) + in2[s, f].astype(jnp.float32)
            )
        return jnp.concatenate(whole, axis=1)

    def send_third(s):
        m = order[s]
        out3[m - 1] = finish(s).astype(jnp.bfloat16)
        third[m] = remote(
            out3.at[m - 1], in3.at[m - 1], s3_send.at[m - 1], s3_recv.at[m - 1], line_ids[m]
        )

    step = 128

    def make_unit(index):
        at = index * step
        ref, begin = (pts, at) if at < local else (sib_pts, at - local)
        wide = ref[begin : begin + step].astype(jnp.float32)
        mean = jnp.mean(wide * wide, axis=1, keepdims=True)
        unit = wide * lax.rsqrt(mean + EPSILON)
        unit_t[:, at : at + step] = unit.T.astype(jnp.bfloat16)

    units = 2 * local // step
    for s in range(chips):
        add_sibling(s)
    made = 0
    for s in range(chips):
        for _ in range(units // chips):
            make_unit(made)
            made += 1
        send_second(s)
        if s + 2 < chips:
            send_first(s + 2, 0)
            send_first(s + 2, 1)
        if s:
            send_third(s - 1)
    total = finish(chips - 1)
    for m in (2, 3, 1):
        third[m].wait_recv()
        total = total + in3[m - 1].astype(jnp.float32)
    mean = jnp.mean(total * total, axis=1, keepdims=True)
    grid[0, c] = (total * lax.rsqrt(mean + EPSILON)).astype(jnp.bfloat16)

    along = [None] * chips
    across = [[None, None] for _ in range(chips)]
    corner = [[None, None] for _ in range(chips)]

    def send_across(m):
        k = line[m]
        for f in range(2):
            across[m][f] = remote(
                grid.at[0, k], grid.at[1 + f, k], g2_send.at[m, f], g2_recv.at[m, f], (x_id, y_id)[f]
            )

    def send_corner(m):
        k = line[m]
        for f in range(2):
            across[m][f].wait_recv()
            corner[m][f] = remote(
                grid.at[1 + f, k, :, halves[f]],
                grid.at[3, k, :, halves[f]],
                g3_send.at[m, f],
                g3_recv.at[m, f],
                (y_id, x_id)[f],
            )

    for m in range(1, chips):
        along[m] = remote(
            grid.at[0, c], grid.at[0, c], g1_send.at[m - 1], g1_recv.at[m - 1], line_ids[m]
        )
    send_across(0)
    for m in range(1, chips):
        along[m].wait_recv()
        send_across(m)
        send_corner(m - 1)

    def best_of(r):
        block = grid[r].reshape(K_HOST, features)
        scores = jnp.dot(block, unit_t[...], preferred_element_type=jnp.float32)
        return jnp.max(scores, axis=0, keepdims=True)

    quarter = features // chips
    columns = pl.ds(pl.multiple_of(c * quarter, quarter), quarter)
    for k in range(chips):
        cent_ref[k * rows : (k + 1) * rows, :] = grid[0, k, :, columns]
    best = best_of(0)
    send_corner(chips - 1)
    for r in (1, 2):
        best = jnp.maximum(best, best_of(r))
    for m in range(chips):
        for f in range(2):
            corner[m][f].wait_recv()
    best = jnp.maximum(best, best_of(3))

    best_out[...] = best[:, local:]
    last = remote(best_out, best_in, core_send.at[3], core_recv.at[3], sibling)
    for copy in started:
        copy.wait_send()
    last.wait_recv()
    near_ref[...] = 2.0 - 2.0 * jnp.maximum(best[:, :local], best_in[...]) / features


def window_body(points, assign):
    local, features = points.shape
    chips = lax.axis_size("chip")
    rows = K_HOST // chips
    half = features // 2
    vmem = pl.BlockSpec(memory_space=pltpu.VMEM)
    anywhere = pl.BlockSpec(memory_space=pl.ANY)
    dma = pltpu.SemaphoreType.DMA
    pieces = [
        pltpu.VMEM((chips, 2, 2, rows, half), jnp.bfloat16),
        pltpu.VMEM((chips, 2, rows, half), jnp.bfloat16),
        pltpu.VMEM((chips - 1, rows, features), jnp.bfloat16),
    ]
    pairs = [(4,), (chips, 2), (chips, 2), (chips - 1,), (chips - 1,), (chips, 2), (chips, 2)]
    centroids, nearest = pl.pallas_call(
        functools.partial(window_kernel, chips),
        out_shape=(
            jax.ShapeDtypeStruct((K_HOST, features // chips), jnp.bfloat16),
            jax.ShapeDtypeStruct((1, local), jnp.float32),
        ),
        in_specs=[anywhere, anywhere],
        out_specs=(vmem, vmem),
        scratch_shapes=[
            pltpu.VMEM((1, local), jnp.int32),
            pltpu.VMEM((local, features), jnp.bfloat16),
            pltpu.VMEM((1, local), jnp.int32),
            pltpu.VMEM((local, features), jnp.bfloat16),
            pltpu.VMEM((chips, QUAD * rows, features), jnp.float32),
            *(buffer for buffer in pieces for _ in range(2)),
            pltpu.VMEM((QUAD, chips, rows, features), jnp.bfloat16),
            pltpu.VMEM((features, 2 * local), jnp.bfloat16),
            pltpu.VMEM((1, local), jnp.float32),
            pltpu.VMEM((1, local), jnp.float32),
            dma((2,)),
            *(dma(shape) for shape in pairs for _ in range(2)),
        ],
        compiler_params=pltpu.CompilerParams(
            collective_id=0, has_side_effects=True, vmem_limit_bytes=48 * 1024 * 1024
        ),
    )(assign.reshape(1, local), points)
    return (centroids, nearest.reshape(local))


def solution(mesh):
    hosts, chips = mesh.shape["hst"], mesh.shape["chip"]
    fits = hosts == CYCLE and hosts == 2 * QUAD and chips == 4
    in_specs = (P(("hst", "chip"), None), P(("hst", "chip")))
    out_specs = (P("hst", "chip"), P(("hst", "chip")))
    return jax.shard_map(
        window_body if fits else general_body,
        mesh=mesh,
        in_specs=in_specs,
        out_specs=out_specs,
        check_vma=False,
    )
```

time: 43.9 us -> 43.5 us (level)
  no operation moved by 1% of the time
where the time goes in v2:
time: 43.5 us; the launch traced here: 43.3 us
  Pallas kernels  39.6 us (91%)
  local copies, waits for them, and re-layouts  3.11 us (7%)
  between operations  0.65 us (1%)
    pallas_call x1, Pallas kernels, window_body(): pl.pallas_call(functools.partial(window_kernel, chips), out_shape=(jax.Sh...  39.6 us
    unnamed x6, local copies, waits for them, and re-layouts  3.11 us

profile of v2, /device:TPU:0, one launch (start us, length us, event | category | flops | bytes accessed | tf_op | source)
XLA Modules:
  0.0 43.3 jit_solution(12321169746045310047)
XLA Ops:
  0.6 0.0 copy-start
  0.6 1.2 %copy-done = bf16[512,1024]{1,0:T(8,128)(2,1)S(1)} copy-done((bf16[512,1024]{1,0:T(8,128)(2,1)S(1)}, bf16[512,1024]{1,0:T(8,128)(2,1)}, u32[]{:S(2)}) %copy-start) | copy-done | bytes 1048600
  1.9 0.0 copy-start.1
  1.9 0.7 %copy-done.1 = s32[512]{0:T(512)S(1)} copy-done((s32[512]{0:T(512)S(1)}, s32[512]{0:T(512)}, u32[]{:S(2)}) %copy-start.1) | copy-done | bytes 2072
  2.5 39.6 %shard_map.41 = (bf16[128,256]{1,0:T(8,128)(2,1)S(1)}, f32[1,512]{1,0:T(1,128)S(1)}) custom-call(s32[1,512]{1,0:T(1,128)S(1)} %bitcast.2, bf16[512,1024]{1,0:T(8,128)(2,1)S(1)} %copy-done), custom_call_target="tpu_custom_call" | custom-call | tf_op jit(solution)/shard_map/pallas_call | solution.py:335
  42.1 0.6 %copy.6 = bf16[128,256]{1,0:T(8,128)(2,1)} copy(bf16[128,256]{1,0:T(8,128)(2,1)S(1)} %get-tuple-element.8) | data formatting | bytes 131072
  42.8 0.6 %copy.7 = f32[512]{0:T(512)} copy(f32[512]{0:T(512)S(1)} %bitcast.3) | data formatting | bytes 4096
Async XLA Ops:
  0.6 1.2 %copy-start = (bf16[512,1024]{1,0:T(8,128)(2,1)S(1)}, bf16[512,1024]{1,0:T(8,128)(2,1)}, u32[]{:S(2)}) copy-start(bf16[512,1024]{1,0:T(8,128)(2,1)} %pts_hbm.1) | copy-start | bytes 3145732
  1.9 0.7 %copy-start.1 = (s32[512]{0:T(512)S(1)}, s32[512]{0:T(512)}, u32[]{:S(2)}) copy-start(s32[512]{0:T(512)} %param.3) | copy-start | bytes 6148

commit v3 on v2

--- a/solution.py
+++ b/solution.py
@@ -77,12 +77,10 @@
 
 def window_kernel(
     chips,
-    lab_hbm,
-    pts_hbm,
+    lab,
+    pts,
     cent_ref,
     near_ref,
-    lab,
-    pts,
     sib_lab,
     sib_pts,
     sums,
@@ -96,7 +94,6 @@
     unit_t,
     best_out,
     best_in,
-    load_sem,
     core_send,
     core_recv,
     s1_send,
@@ -109,8 +106,6 @@
     g1_recv,
     g2_send,
     g2_recv,
-    g3_send,
-    g3_recv,
 ):
     local, features = pts.shape
     rows = K_HOST // chips
@@ -123,18 +118,15 @@
     qx, qy = quad % 2, quad // 2
     sibling = (h + 1 - 2 * core, c)
     quads = [quad, qy * 2 + (1 - qx), (1 - qy) * 2 + qx, (1 - qy) * 2 + (1 - qx)]
-    x_id, y_id = [(quads[r] * 2 + core, c) for r in (1, 2)]
+    quad_ids = [(q * 2 + core, c) for q in quads]
+    x_id, y_id = quad_ids[1:3]
     line = [c, c + 1 - 2 * (c % 2), (c + 2) % 4, 3 - c]
     line_ids = [(h, k) for k in line]
 
     barrier = pltpu.get_barrier_semaphore()
-    partners = [sibling, x_id, y_id] + line_ids[1:]
+    partners = [sibling] + quad_ids[1:] + line_ids[1:]
     for partner in partners:
         pl.semaphore_signal(barrier, inc=1, device_id=partner, device_id_type=MESH)
-    lab_load = pltpu.make_async_copy(lab_hbm, lab, load_sem.at[0])
-    lab_load.start()
-    pts_load = pltpu.make_async_copy(pts_hbm, pts, load_sem.at[1])
-    pts_load.start()
     pl.semaphore_wait(barrier, len(partners))
 
     started = []
@@ -152,10 +144,10 @@
         started.append(copy)
         return copy
 
-    lab_swap = remote(lab_hbm, sib_lab, core_send.at[0], core_recv.at[0], sibling)
+    lab_swap = remote(lab, sib_lab, core_send.at[0], core_recv.at[0], sibling)
     pts_swap = [
         remote(
-            pts_hbm.at[:, halves[f]], sib_pts.at[:, halves[f]], core_send.at[1 + f], core_recv.at[1 + f], sibling
+            pts.at[:, halves[f]], sib_pts.at[:, halves[f]], core_send.at[1 + f], core_recv.at[1 + f], sibling
         )
         for f in range(2)
     ]
@@ -171,8 +163,6 @@
     def members(s, labels):
         return (base + line[order[s]] * rows == labels[...]).astype(jnp.bfloat16)
 
-    lab_load.wait()
-    pts_load.wait()
     for s in range(chips):
         sums[s] = jnp.dot(members(s, lab), pts[...], preferred_element_type=jnp.float32)
     lab_swap.wait_recv()
@@ -260,37 +250,23 @@
     grid[0, c] = (total * lax.rsqrt(mean + EPSILON)).astype(jnp.bfloat16)
 
     along = [None] * chips
-    across = [[None, None] for _ in range(chips)]
-    corner = [[None, None] for _ in range(chips)]
+    across = [[None] * QUAD for _ in range(chips)]
 
     def send_across(m):
         k = line[m]
-        for f in range(2):
-            across[m][f] = remote(
-                grid.at[0, k], grid.at[1 + f, k], g2_send.at[m, f], g2_recv.at[m, f], (x_id, y_id)[f]
+        for r in (3, 1, 2):
+            across[m][r] = remote(
+                grid.at[0, k], grid.at[r, k], g2_send.at[m, r - 1], g2_recv.at[m, r - 1], quad_ids[r]
             )
 
-    def send_corner(m):
-        k = line[m]
-        for f in range(2):
-            across[m][f].wait_recv()
-            corner[m][f] = remote(
-                grid.at[1 + f, k, :, halves[f]],
-                grid.at[3, k, :, halves[f]],
-                g3_send.at[m, f],
-                g3_recv.at[m, f],
-                (y_id, x_id)[f],
-            )
-
-    for m in range(1, chips):
+    for m in (2, 1, 3):
         along[m] = remote(
             grid.at[0, c], grid.at[0, c], g1_send.at[m - 1], g1_recv.at[m - 1], line_ids[m]
         )
     send_across(0)
-    for m in range(1, chips):
+    for m in (1, 2, 3):
         along[m].wait_recv()
         send_across(m)
-        send_corner(m - 1)
 
     def best_of(r):
         block = grid[r].reshape(K_HOST, features)
@@ -302,13 +278,10 @@
     for k in range(chips):
         cent_ref[k * rows : (k + 1) * rows, :] = grid[0, k, :, columns]
     best = best_of(0)
-    send_corner(chips - 1)
-    for r in (1, 2):
+    for r in (1, 2, 3):
+        for m in range(chips):
+            across[m][r].wait_recv()
         best = jnp.maximum(best, best_of(r))
-    for m in range(chips):
-        for f in range(2):
-            corner[m][f].wait_recv()
-    best = jnp.maximum(best, best_of(3))
 
     best_out[...] = best[:, local:]
     last = remote(best_out, best_in, core_send.at[3], core_recv.at[3], sibling)
@@ -324,25 +297,22 @@
     rows = K_HOST // chips
     half = features // 2
     vmem = pl.BlockSpec(memory_space=pltpu.VMEM)
-    anywhere = pl.BlockSpec(memory_space=pl.ANY)
     dma = pltpu.SemaphoreType.DMA
     pieces = [
         pltpu.VMEM((chips, 2, 2, rows, half), jnp.bfloat16),
         pltpu.VMEM((chips, 2, rows, half), jnp.bfloat16),
         pltpu.VMEM((chips - 1, rows, features), jnp.bfloat16),
     ]
-    pairs = [(4,), (chips, 2), (chips, 2), (chips - 1,), (chips - 1,), (chips, 2), (chips, 2)]
+    pairs = [(4,), (chips, 2), (chips, 2), (chips - 1,), (chips - 1,), (chips, 3)]
     centroids, nearest = pl.pallas_call(
         functools.partial(window_kernel, chips),
         out_shape=(
             jax.ShapeDtypeStruct((K_HOST, features // chips), jnp.bfloat16),
             jax.ShapeDtypeStruct((1, local), jnp.float32),
         ),
-        in_specs=[anywhere, anywhere],
+        in_specs=[vmem, vmem],
         out_specs=(vmem, vmem),
         scratch_shapes=[
-            pltpu.VMEM((1, local), jnp.int32),
-            pltpu.VMEM((local, features), jnp.bfloat16),
             pltpu.VMEM((1, local), jnp.int32),
             pltpu.VMEM((local, features), jnp.bfloat16),
             pltpu.VMEM((chips, QUAD * rows, features), jnp.float32),
@@ -351,7 +321,6 @@
             pltpu.VMEM((features, 2 * local), jnp.bfloat16),
             pltpu.VMEM((1, local), jnp.float32),
             pltpu.VMEM((1, local), jnp.float32),
-            dma((2,)),
             *(dma(shape) for shape in pairs for _ in range(2)),
         ],
         compiler_params=pltpu.CompilerParams(

time: 43.5 us -> 41.8 us (0.961)
  Pallas kernels: 39.6 us -> 37.6 us
    pallas_call x1, Pallas kernels: 39.6 us -> 37.6 us  [window_body(): pl.pallas_call(functools.partial(window_kernel, chips), out_shape=(jax.Sh...]
where the time goes in v3:
time: 41.8 us; the launch traced here: 41.4 us
  Pallas kernels  37.6 us (90%)
  local copies, waits for them, and re-layouts  3.11 us (7%)
  between operations  0.65 us (2%)
    pallas_call x1, Pallas kernels, window_body(): pl.pallas_call(functools.partial(window_kernel, chips), out_shape=(jax.Sh...  37.6 us
    unnamed x6, local copies, waits for them, and re-layouts  3.11 us

profile of v3, /device:TPU:0, one launch (start us, length us, event | category | flops | bytes accessed | tf_op | source)
XLA Modules:
  0.0 41.4 jit_solution(5339802624340934204)
XLA Ops:
  0.6 0.0 copy-start
  0.6 1.2 %copy-done = bf16[512,1024]{1,0:T(8,128)(2,1)S(1)} copy-done((bf16[512,1024]{1,0:T(8,128)(2,1)S(1)}, bf16[512,1024]{1,0:T(8,128)(2,1)}, u32[]{:S(2)}) %copy-start) | copy-done | bytes 1048600
  1.9 0.0 copy-start.1
  1.9 0.7 %copy-done.1 = s32[512]{0:T(512)S(1)} copy-done((s32[512]{0:T(512)S(1)}, s32[512]{0:T(512)}, u32[]{:S(2)}) %copy-start.1) | copy-done | bytes 2072
  2.5 37.6 %shard_map.41 = (bf16[128,256]{1,0:T(8,128)(2,1)S(1)}, f32[1,512]{1,0:T(1,128)S(1)}) custom-call(s32[1,512]{1,0:T(1,128)S(1)} %bitcast.2, bf16[512,1024]{1,0:T(8,128)(2,1)S(1)} %copy-done), custom_call_target="tpu_custom_call" | custom-call | tf_op jit(solution)/shard_map/pallas_call | solution.py:307
  40.2 0.6 %copy.6 = bf16[128,256]{1,0:T(8,128)(2,1)} copy(bf16[128,256]{1,0:T(8,128)(2,1)S(1)} %get-tuple-element.8) | data formatting | bytes 131072
  40.8 0.6 %copy.7 = f32[512]{0:T(512)} copy(f32[512]{0:T(512)S(1)} %bitcast.3) | data formatting | bytes 4096
Async XLA Ops:
  0.6 1.2 %copy-start = (bf16[512,1024]{1,0:T(8,128)(2,1)S(1)}, bf16[512,1024]{1,0:T(8,128)(2,1)}, u32[]{:S(2)}) copy-start(bf16[512,1024]{1,0:T(8,128)(2,1)} %pts.1) | copy-start | bytes 3145732
  1.9 0.7 %copy-start.1 = (s32[512]{0:T(512)S(1)}, s32[512]{0:T(512)}, u32[]{:S(2)}) copy-start(s32[512]{0:T(512)} %param.3) | copy-start | bytes 6148

commit v4 on v3

--- a/solution.py
+++ b/solution.py
@@ -233,13 +233,13 @@
         add_sibling(s)
     made = 0
     for s in range(chips):
-        for _ in range(units // chips):
-            make_unit(made)
-            made += 1
         send_second(s)
         if s + 2 < chips:
             send_first(s + 2, 0)
             send_first(s + 2, 1)
+        for _ in range(units // chips):
+            make_unit(made)
+            made += 1
         if s:
             send_third(s - 1)
     total = finish(chips - 1)

time: 41.8 us -> 41.8 us (level)
  no operation moved by 1% of the time
where the time goes in v4:
time: 41.8 us; the launch traced here: 41.4 us
  Pallas kernels  37.6 us (90%)
  local copies, waits for them, and re-layouts  3.11 us (7%)
  between operations  0.65 us (2%)
    pallas_call x1, Pallas kernels, window_body(): pl.pallas_call(functools.partial(window_kernel, chips), out_shape=(jax.Sh...  37.6 us
    unnamed x6, local copies, waits for them, and re-layouts  3.11 us

profile of v4, /device:TPU:0, one launch (start us, length us, event | category | flops | bytes accessed | tf_op | source)
XLA Modules:
  0.0 41.4 jit_solution(543926835804826561)
XLA Ops:
  0.6 0.0 copy-start
  0.6 1.2 %copy-done = bf16[512,1024]{1,0:T(8,128)(2,1)S(1)} copy-done((bf16[512,1024]{1,0:T(8,128)(2,1)S(1)}, bf16[512,1024]{1,0:T(8,128)(2,1)}, u32[]{:S(2)}) %copy-start) | copy-done | bytes 1048600
  1.9 0.0 copy-start.1
  1.9 0.7 %copy-done.1 = s32[512]{0:T(512)S(1)} copy-done((s32[512]{0:T(512)S(1)}, s32[512]{0:T(512)}, u32[]{:S(2)}) %copy-start.1) | copy-done | bytes 2072
  2.5 37.6 %shard_map.41 = (bf16[128,256]{1,0:T(8,128)(2,1)S(1)}, f32[1,512]{1,0:T(1,128)S(1)}) custom-call(s32[1,512]{1,0:T(1,128)S(1)} %bitcast.2, bf16[512,1024]{1,0:T(8,128)(2,1)S(1)} %copy-done), custom_call_target="tpu_custom_call" | custom-call | tf_op jit(solution)/shard_map/pallas_call | solution.py:307
  40.2 0.6 %copy.6 = bf16[128,256]{1,0:T(8,128)(2,1)} copy(bf16[128,256]{1,0:T(8,128)(2,1)S(1)} %get-tuple-element.8) | data formatting | bytes 131072
  40.8 0.6 %copy.7 = f32[512]{0:T(512)} copy(f32[512]{0:T(512)S(1)} %bitcast.3) | data formatting | bytes 4096
Async XLA Ops:
  0.6 1.2 %copy-start = (bf16[512,1024]{1,0:T(8,128)(2,1)S(1)}, bf16[512,1024]{1,0:T(8,128)(2,1)}, u32[]{:S(2)}) copy-start(bf16[512,1024]{1,0:T(8,128)(2,1)} %pts.1) | copy-start | bytes 3145732
  1.9 0.7 %copy-start.1 = (s32[512]{0:T(512)S(1)}, s32[512]{0:T(512)}, u32[]{:S(2)}) copy-start(s32[512]{0:T(512)} %param.3) | copy-start | bytes 6148
